TPU v7x, 32 devices: a whole 2x2x4 slice. The times are simulated.
32 devices in a mesh: flow: 8 (over z, x), cross: 4 (over y, core).
Axes of the slice: x: 2, y: 2, z: 4, core: 2. Of those that a mesh axis runs over, the one named last changes fastest.
Arguments:
- particles: float32 [1536, 8, 128], P(('flow', 'cross')), may hold values from -1.5 to 48, as said below
- counts: int32 [1536], P(('flow', 'cross')), may hold values from 32 to 128, as said below
- pairs: int32 [1536, 45], P(('flow', 'cross')), may hold values from 0 to 959, as said below
Outputs:
- rates: float32 [1536, 4, 128], P(('flow', 'cross'))
Inputs may be any that keep to these rules, and one draw needn't show every extreme that they name: `particles`: each block holds one cell of 1 x 2 x 2 (cells have y index in 0 to 7 and z index in 0 to 23); which cell a block holds follows one order, the same in every slab; positions lie inside their cell; density between 0.9 and 1.1, positive masses. `counts`: some block is full. `pairs`: the codes of a block name the blocks of its own cell and of its neighbour cells within one cell across (periodic) and two slabs along the flow.
All inputs are finite; a program needn't handle non-finite values.
Results may differ from a plain program's by a relative error of at most 0.0003.
Values sent between devices are 32-bit elements; how exact they have to be, the bound alone decides.
A program may use at most 64 MiB of HBM per device.

v0:
```python
import functools
import math

import jax
import jax.numpy as jnp
from jax import lax
from jax.experimental import pallas as pl
from jax.experimental.pallas import tpu as pltpu
from jax.sharding import PartitionSpec as P

GY = 8


kernel_coef = 5.0 * 21.0 / (16.0 * math.pi)
eta_square = 0.01
sound_speed = 6.0
delta_coef = 0.1
visc_coef = 0.1
slab_order = (-2, -1, 0, 1, 2)
wave = sound_speed * visc_coef
stiff = sound_speed / visc_coef
rows_step = 16
tail_step = 4
fields = 7


def passed_along(value, axis, steps):
    count = lax.axis_size(axis)
    pairs = [(source, (source + steps) % count) for source in range(count)]
    return lax.ppermute(value, axis, pairs)


def in_order(codes):
    places = jnp.arange(codes.shape[1], dtype=jnp.int32)
    mine, other = codes[:, :, None], codes[:, None, :]
    before = (other < mine) | ((other == mine) & (places[None, None, :] < places[None, :, None]))
    rank = jnp.sum(before.astype(jnp.int32), axis=2)
    return jnp.sum(jnp.where(rank[:, None, :] == places[None, :, None], codes[:, None, :], 0), axis=2)


def ready_kernel(counts, particles, out):
    blocks, width, slots = particles.shape
    lanes = lax.broadcasted_iota(jnp.int32, (1, slots), 1)

    def one(block, unused):
        rho = particles[block, 6:7, :]
        out[block, 0:6, :] = particles[block, 0:6, :]
        out[block, 6:7, :] = stiff * (rho - 1.0)
        out[block, 7:8, :] = jnp.where(lanes < counts[block], particles[block, 7:8, :] / rho, 0.0)
        return unused

    lax.fori_loop(0, blocks, one, 0, unroll=8)


def pair_kernel(main_step, slabs, per_slab, wide_y, wide_z, codes, live_counts, source_counts, ready, lookup, *rest_refs):
    spread, rest_refs = rest_refs[:fields], rest_refs[fields:]
    earlier = rest_refs[0] if len(rest_refs) == 5 else None
    particles, out, packed, totals = rest_refs[-4:]
    block = pl.program_id(0)
    blocks, width, slots = ready.shape
    lanes = lax.broadcasted_iota(jnp.int32, (8, slots), 1)
    row = lax.broadcasted_iota(jnp.int32, (8, slots), 0)
    wide = jnp.where(row == 1, wide_y, jnp.where(row == 2, wide_z, 0.0))
    inverse = jnp.where(row == 1, 1.0 / wide_y, jnp.where(row == 2, 1.0 / wide_z, 0.0))
    along = jnp.where(row == 0, 1.0, 0.0)
    empty = jnp.zeros((8, slots), jnp.float32)
    scale = kernel_coef / 8.0
    def finish(block):
        every = totals[...]
        high = every.astype(jnp.bfloat16)
        low = (every - high.astype(jnp.float32)).astype(jnp.bfloat16)
        ones = jnp.ones((2 * slots, slots), jnp.bfloat16)
        every = jnp.dot(jnp.concatenate([high, low], axis=1), ones, preferred_element_type=jnp.float32)
        rows = []
        for which in range(5):
            total = empty
            for group in range(slots // 8):
                begin = which * slots + group * 8
                total = total + jnp.where(lanes == row + group * 8, every[begin:begin + 8], 0.0)
            rows.append(jnp.sum(total, axis=0, keepdims=True))
        rho = particles[block, 6:7, :]
        drho = scale * (2.0 * delta_coef * sound_speed / stiff * rows[1] - rho * rows[0])
        over = (scale * wave) / rho
        alive = lanes[0:1] < live_counts[block]
        results = [drho] + [over * rows[2 + axis] for axis in range(3)]
        for place, result in enumerate(results):
            if earlier is not None:
                result = result + earlier[block, place:place + 1, :]
            out[block, place:place + 1, :] = jnp.where(alive, result, 0.0)

    finish(jnp.maximum(block - 1, 0))
    own = ready[block]
    own_first = jnp.broadcast_to(own[:, 0:1], (8, slots)) * inverse + 0.5

    current, tile, start = empty, jnp.int32(0), jnp.int32(0)
    shifts = []
    for step in range(len(slabs) * per_slab):
        slab, cell = divmod(step, per_slab)
        code = codes[block * (len(slabs) * per_slab) + step]
        count = source_counts[code]
        value = lookup[code]
        if slab == 0:
            first = jnp.broadcast_to(value[:, 0:1], (8, slots))
            shifts.append(wide * jnp.floor(own_first - first * inverse))
        value = value + (shifts[cell] + along * slabs[slab])
        turned = pltpu.roll(value, start, 1)
        ahead = lanes >= start
        merged = jnp.where(ahead, turned, current)
        packed[tile] = merged
        end = start + count
        full = (end >= slots).astype(jnp.int32)
        keep = jnp.broadcast_to(full, (8, slots)) == 0
        rest = jnp.where(ahead, 0.0, turned)
        current = jnp.where(keep, merged, rest)
        tile = tile + full
        start = end - full * slots
    packed[tile] = current
    for more in range(1, tail_step):
        packed[tile + more] = empty
    tiles = tile + (start > 0).astype(jnp.int32)
    live = live_counts[block]

    def per_rows(index, unused):
        first = pl.multiple_of(index * rows_step, rows_step)
        rows = pl.ds(first, rows_step)
        xi, yi, zi, ui, vi, wi, pi = [spread[field][0, 0, rows, :] for field in range(fields)]

        def one_tile(place, sums):
            s_close, s_diff, s_damp, s_x, s_y, s_z = sums
            xj, yj, zj, uj, vj, wj, pj, volume = [packed[place, field:field + 1, :] for field in range(8)]
            gap_x = xi - xj
            gap_y = yi - yj
            gap_z = zi - zj
            shifted = (gap_x * gap_x + eta_square) + (gap_y * gap_y + gap_z * gap_z)
            inv = lax.rsqrt(shifted)
            bump = jnp.maximum(2.0 - shifted * inv, 0.0)
            weight = (bump * bump) * (bump * volume)
            closing = (ui - uj) * gap_x + (vi - vj) * gap_y + (wi - wj) * gap_z
            inv_sq = inv * inv
            diff = weight * (pj - pi)
            push = weight * ((pi + pj) - closing * inv_sq)
            return (
                s_close + weight * closing,
                s_diff + diff,
                s_damp + diff * inv_sq,
                s_x + push * gap_x,
                s_y + push * gap_y,
                s_z + push * gap_z,
            )

        sums = (jnp.zeros((rows_step, slots), jnp.float32),) * 6
        def some_tiles(step, begin):
            def body(turn, sums):
                for more in range(step):
                    sums = one_tile(begin + turn * step + more, sums)
                return sums
            return body

        turns = (tiles + tail_step - 1) // main_step
        begin = turns * main_step
        tails = (jnp.maximum(tiles - begin, 0) + tail_step - 1) // tail_step
        sums = lax.fori_loop(0, turns, some_tiles(main_step, 0), sums)
        sums = lax.fori_loop(0, tails, some_tiles(tail_step, begin), sums)
        kept = (sums[0], sums[1] - eta_square * sums[2], sums[3], sums[4], sums[5])
        for which in range(5):
            totals[pl.ds(pl.multiple_of(which * slots + first, rows_step), rows_step), :] = kept[which]
        return unused

    lax.fori_loop(0, (live + rows_step - 1) // rows_step, per_rows, 0)

    @pl.when(block == blocks - 1)
    def _():
        finish(block)


def per_device(particles, counts, pairs):
    blocks, width, slots = particles.shape
    slab_blk = blocks * lax.axis_size("cross")
    cells_z = slab_blk // GY
    per_block = pairs.shape[1]
    vmem = pl.BlockSpec(memory_space=pltpu.VMEM)
    smem = pl.BlockSpec(memory_space=pltpu.SMEM)
    limit = pltpu.CompilerParams(vmem_limit_bytes=40 * 1024 * 1024)
    ready = pl.pallas_call(
        ready_kernel,
        out_shape=jax.ShapeDtypeStruct(particles.shape, jnp.float32),
        in_specs=[smem, vmem],
        out_specs=vmem,
        compiler_params=limit,
        name="ready",
    )(counts, particles)
    nearby = {offset: passed_along(ready, "flow", -offset) for offset in (-2, 2, -1)}
    spread = jnp.broadcast_to(ready[:, :fields, :, None], (blocks, fields, slots, slots))
    spread, held = lax.optimization_barrier((spread, ready))
    nearby[1] = passed_along(held, "flow", -1)
    listed = in_order(pairs)
    per_slab = per_block // len(slab_order)
    middle = per_slab * (len(slab_order) // 2)
    own_codes = listed[:, middle:middle + per_slab] - 2 * slab_blk
    far_codes = jnp.concatenate([listed[:, :middle], listed[:, middle + per_slab:] - slab_blk], axis=1)
    own_lookup = lax.all_gather(ready, "cross", axis=0, tiled=True)
    stacked = jnp.stack([nearby[offset] for offset in slab_order if offset])
    stacked, own_lookup = lax.optimization_barrier((stacked, own_lookup))
    far_lookup = lax.all_gather(stacked, "cross", axis=1, tiled=True)
    far_lookup = far_lookup.reshape((4 * slab_blk, width, slots))


    def rates(main_step, slabs, codes, lookup, more, name):
        slot_ids = jnp.arange(slots, dtype=jnp.int32)
        source_counts = jnp.max(jnp.where(lookup[:, 7] > 0.0, slot_ids[None, :] + 1, 0), axis=1)
        work = blocks * slots * slots * len(slabs) * per_slab
        return pl.pallas_call(
            functools.partial(pair_kernel, main_step, slabs, per_slab, 2.0 * GY, 2.0 * cells_z),
            out_shape=jax.ShapeDtypeStruct((blocks, 4, slots), jnp.float32),
            grid=(blocks,),
            in_specs=[smem, smem, smem, vmem, vmem]
            + [pl.BlockSpec((1, 1, slots, slots), lambda i, field=field: (i, field, 0, 0)) for field in range(fields)]
            + [vmem] * (len(more) + 1),
            out_specs=vmem,
            scratch_shapes=[
                pltpu.VMEM((len(slabs) * per_slab + main_step + tail_step, 8, slots), jnp.float32),
                pltpu.VMEM((5 * slots, slots), jnp.float32),
            ],
            compiler_params=limit,
            cost_estimate=pl.CostEstimate(flops=60 * work, bytes_accessed=4 * lookup.size, transcendentals=work),
            name=name,
        )(codes.reshape(-1), counts, source_counts, ready, lookup, *(fields * [spread]), *more, particles)

    own_rates = rates(8, (0.0,), own_codes, own_lookup, (), "own_slab")
    far_slabs = tuple(float(offset) for offset in slab_order if offset)
    return rates(12, far_slabs, far_codes, far_lookup, (own_rates,), "other_slabs")


def solution(mesh):
    placed = (P(("flow", "cross"), None, None), P(("flow", "cross")), P(("flow", "cross"), None))
    return jax.shard_map(
        per_device,
        mesh=mesh,
        in_specs=placed,
        out_specs=P(("flow", "cross"), None, None),
        check_vma=False,
    )
```

profile of v0, /device:TPU:9, one launch (start us, length us, event | category | flops | bytes accessed | tf_op | source)
XLA Modules:
  0.0 206.3 jit_solution(3217167690439311539)
XLA Ops:
  6.5 0.0 all-gather.2.cloned.1.call-start
  6.5 0.0 copy-start.1
  6.5 0.9 copy-done.1
  7.5 0.0 copy-start.3
  7.5 0.7 copy-done.3
  8.1 0.6 ready.1
  8.8 1.3 collective-permute-start
  10.1 1.2 collective-permute-start.1
  11.3 0.2 collective-permute-start.3
  11.5 7.9 %broadcast_in_dim.50.rest_refs_0_.rest_refs_1_.rest_refs_2_.rest_refs_3_.rest_refs_4_.rest_refs_5_.rest_refs_6_ = f32[48,7,128,128]{3,2,1,0:T(8,128)} broadcast(f32[48,7,128]{2,1,0:T(8,128)S(1)} %bitcast.12), dimensions={0,1,2} | broadcast | bytes 22192128 | tf_op jit(solution)/shard_map/broadcast_in_dim | solution.py:193
  19.4 3.0 %collective-permute-start.2 = (f32[48,8,128]{2,1,0:T(8,128)S(1)}, f32[48,8,128]{2,1,0:T(8,128)S(1)}, u32[]{:S(2)}, u32[]{:S(2)}) collective-permute-start(f32[48,8,128]{2,1,0:T(8,128)S(1)} %ready.1), channel_id=1, source_target_pairs={{0,28},{4,0},{8,4},{12,8},{16,12},{20,16},{24,20},{28,24},{1,29},{... | collective-permute-start | bytes 589832 | tf_op jit(solution)/shard_map/ppermute | solution.py:30
  22.4 10.2 %all_gather.6.lookup = f32[192,8,128]{2,1,0:T(8,128)S(1)} all-gather(f32[48,8,128]{2,1,0:T(8,128)S(1)} %ready.1), channel_id=1, replica_groups=mesh['flow'=8,'cross'=4] {'cross'}, dimensions={0}, use_global_device_ids=true | all-gather | bytes 983040 | tf_op jit(solution)/shard_map/all_gather | solution.py:201
  32.6 0.0 collective-permute-done.2
  32.6 0.0 collective-permute-done
  32.6 0.0 collective-permute-done.1
  32.7 0.0 collective-permute-done.3
  32.7 0.0 copy-start.5
  32.7 1.0 pad_maximum_fusion
  33.7 0.0 all-gather.2.cloned.1.call-update
  33.7 0.0 copy-done.5
  33.7 0.0 copy-start.2
  33.7 0.0 copy-start.4
  33.7 0.1 copy.5
  33.8 0.6 convert_reduce_fusion
  34.4 0.2 select_reduce_fusion
  34.6 0.1 copy.8
  34.7 0.1 reshape.39.codes
  34.9 0.1 copy.7
  34.9 0.1 reshape.37.codes
  35.1 0.2 copy.9
  35.2 0.1 select_reduce_fusion.2.source_counts
  35.3 0.0 copy-done.2
  35.3 0.0 copy-done.4
  35.4 53.2 %own_slab.1.rest_refs_7_ = f32[48,4,128]{2,1,0:T(4,128)S(1)} custom-call(s32[432]{0:T(512)S(1)} %reshape.39.codes, s32[48]{0:T(128)S(1)} %copy-done.4, s32[192]{0:T(256)S(1)} %select_reduce_fusion.2.source_counts, f32[48,8,128]{2,1,0:T(8,128)S(1)} %ready.1, f32[192,8,128]{2,1,0:T(8,128)S(1)} %all_gather.6.lookup, ...), custom_call_target="tpu_custom_call" | custom-call | flops 424673280 | bytes 786432 | tf_op jit(solution)/shard_map/own_slab/pallas_call | solution.py:212
  88.6 0.0 all-gather.2.cloned.1.call-done
  88.6 2.5 %slice_compare_fusion = pred[768,1,128]{2,1,0:T(4,128)(4,1)S(1)} fusion(f32[768,8,128]{2,1,0:T(8,128)} %bitcast.13), kind=kLoop, calls=%fused_computation.4 | loop fusion | flops 98304 | bytes 491520 | tf_op jit(solution)/shard_map/gt | solution.py:210
  91.1 0.2 select_reduce_fusion.1.source_counts
  91.3 0.0 copy-start
  91.3 1.9 copy-done
  93.2 106.2 %other_slabs.1 = f32[48,4,128]{2,1,0:T(4,128)} custom-call(s32[1728]{0:T(1024)S(1)} %reshape.37.codes, s32[48]{0:T(128)S(1)} %copy-done.4, s32[768]{0:T(1024)S(1)} %select_reduce_fusion.1.source_counts, f32[48,8,128]{2,1,0:T(8,128)S(1)} %ready.1, f32[768,8,128]{2,1,0:T(8,128)S(1)} %bitcast.14, ...), custom_call_target="tpu_custom_call" | custom-call | flops 1698693120 | bytes 3145728 | tf_op jit(solution)/shard_map/other_slabs/pallas_call | solution.py:212
  (5 shorter events, 0.0 us)
Async XLA Ops:
  6.5 82.1 %all-gather.2.cloned.1.call-start = ((), (), s32[]{:S(2)}) async-start(), calls=%async_computation | async-start | bytes 3932160 | tf_op jit(solution)/shard_map/all_gather | solution.py:204
  6.5 0.9 copy-start.1
  7.5 0.7 copy-start.3
  8.8 23.9 %collective-permute-start = (f32[48,8,128]{2,1,0:T(8,128)S(1)}, f32[48,8,128]{2,1,0:T(8,128)S(1)}, u32[]{:S(2)}, u32[]{:S(2)}) collective-permute-start(f32[48,8,128]{2,1,0:T(8,128)S(1)} %ready.1), channel_id=1, source_target_pairs={{0,8},{4,12},{8,16},{12,20},{16,24},{20,28},{24,0},{28,4},{1,9},{5... | collective-permute-start | bytes 589832 | tf_op jit(solution)/shard_map/ppermute | solution.py:30
  10.1 22.5 %collective-permute-start.1 = (f32[48,8,128]{2,1,0:T(8,128)S(1)}, f32[48,8,128]{2,1,0:T(8,128)S(1)}, u32[]{:S(2)}, u32[]{:S(2)}) collective-permute-start(f32[48,8,128]{2,1,0:T(8,128)S(1)} %ready.1), channel_id=1, source_target_pairs={{0,4},{4,8},{8,12},{12,16},{16,20},{20,24},{24,28},{28,0},{1,5},{5... | collective-permute-start | bytes 589832 | tf_op jit(solution)/shard_map/ppermute | solution.py:30
  11.3 21.3 %collective-permute-start.3 = (f32[48,8,128]{2,1,0:T(8,128)S(1)}, f32[48,8,128]{2,1,0:T(8,128)S(1)}, u32[]{:S(2)}, u32[]{:S(2)}) collective-permute-start(f32[48,8,128]{2,1,0:T(8,128)S(1)} %ready.1), channel_id=1, source_target_pairs={{0,24},{4,28},{8,0},{12,4},{16,8},{20,12},{24,16},{28,20},{1,25},{... | collective-permute-start | bytes 589832 | tf_op jit(solution)/shard_map/ppermute | solution.py:30
  19.4 13.2 %collective-permute-start.2 = (f32[48,8,128]{2,1,0:T(8,128)S(1)}, f32[48,8,128]{2,1,0:T(8,128)S(1)}, u32[]{:S(2)}, u32[]{:S(2)}) collective-permute-start(f32[48,8,128]{2,1,0:T(8,128)S(1)} %ready.1), channel_id=1, source_target_pairs={{0,28},{4,0},{8,4},{12,8},{16,12},{20,16},{24,20},{28,24},{1,29},{... | collective-permute-start | bytes 589832 | tf_op jit(solution)/shard_map/ppermute | solution.py:30
  32.7 1.0 copy-start.5
  33.7 1.6 copy-start.2
  33.7 1.6 copy-start.4
  91.3 1.9 copy-start
Sparse Core Ops, SparseCore 0:
  33.8 25.9 all-gather.1
where the time goes:
time: 210 us; the launch traced here: 206 us
  Pallas kernels  160 us (76%)
  between operations  13.6 us (6%)
  local copies, waits for them, and re-layouts  12.1 us (6%)
  blocking collectives  10.2 us (5%)
  starting transfers between devices  5.68 us (3%)
  other arithmetic  4.58 us (2%)
    pallas_call x2, Pallas kernels, rates(): pl.pallas_call(functools.partial(pair_kernel, main_step, slabs, per_slab,...  159 us
    all_gather x1, blocking collectives, per_device(): own_lookup = lax.all_gather(ready, 'cross', axis=0, tiled=True)  10.2 us
    broadcast_in_dim x1, local copies, waits for them, and re-layouts, per_device(): jnp.broadcast_to(ready[:, :fields, :, None], (blocks, fields, slots, slots))  7.94 us
    ppermute x4, starting transfers between devices, passed_along(): return lax.ppermute(value, axis, pairs)  5.68 us
  transfers between devices with their start and end apart: 5, of which 0 were waited for; matrix products, arithmetic and copies ran while one was open for 5% of the time, Pallas kernels for 26%

commit v1 on v0

--- a/solution.py
+++ b/solution.py
@@ -195,15 +195,10 @@
     nearby[1] = passed_along(held, "flow", -1)
     listed = in_order(pairs)
     per_slab = per_block // len(slab_order)
-    middle = per_slab * (len(slab_order) // 2)
-    own_codes = listed[:, middle:middle + per_slab] - 2 * slab_blk
-    far_codes = jnp.concatenate([listed[:, :middle], listed[:, middle + per_slab:] - slab_blk], axis=1)
-    own_lookup = lax.all_gather(ready, "cross", axis=0, tiled=True)
-    stacked = jnp.stack([nearby[offset] for offset in slab_order if offset])
-    stacked, own_lookup = lax.optimization_barrier((stacked, own_lookup))
-    far_lookup = lax.all_gather(stacked, "cross", axis=1, tiled=True)
-    far_lookup = far_lookup.reshape((4 * slab_blk, width, slots))
-
+    nearby[0] = ready
+    stacked = jnp.stack([nearby[offset] for offset in slab_order])
+    everyone = lax.all_gather(stacked, "cross", axis=1, tiled=True)
+    everyone = everyone.reshape((len(slab_order) * slab_blk, width, slots))
 
     def rates(main_step, slabs, codes, lookup, more, name):
         slot_ids = jnp.arange(slots, dtype=jnp.int32)
@@ -226,9 +221,7 @@
             name=name,
         )(codes.reshape(-1), counts, source_counts, ready, lookup, *(fields * [spread]), *more, particles)
 
-    own_rates = rates(8, (0.0,), own_codes, own_lookup, (), "own_slab")
-    far_slabs = tuple(float(offset) for offset in slab_order if offset)
-    return rates(12, far_slabs, far_codes, far_lookup, (own_rates,), "other_slabs")
+    return rates(12, tuple(float(offset) for offset in slab_order), listed, everyone, (), "all_slabs")
 
 
 def solution(mesh):

time: 210 us -> 209 us (level)
  the two profiles are of different devices: /device:TPU:9 before, /device:TPU:2 now
where the time goes in v1:
time: 209 us; the launch traced here: 206 us
  Pallas kernels  132 us (63%)
  waiting for transfers between devices  38.2 us (18%)
  between operations  13.6 us (7%)
  local copies, waits for them, and re-layouts  13 us (6%)
  starting transfers between devices  5.9 us (3%)
  other arithmetic  3.87 us (2%)
    pallas_call x1, Pallas kernels, rates(): pl.pallas_call(functools.partial(pair_kernel, main_step, slabs, per_slab,...  131 us
    all_gather x1, waiting for transfers between devices, per_device(): everyone = lax.all_gather(stacked, 'cross', axis=1, tiled=True)  32 us
    broadcast_in_dim x1, local copies, waits for them, and re-layouts, per_device(): jnp.broadcast_to(ready[:, :fields, :, None], (blocks, fields, slots, slots))  7.97 us
    ppermute x4, waiting for transfers between devices, passed_along(): return lax.ppermute(value, axis, pairs)  6.14 us
    ppermute x4, starting transfers between devices, passed_along(): return lax.ppermute(value, axis, pairs)  5.9 us
    unnamed x19, local copies, waits for them, and re-layouts  4.79 us
  transfers between devices with their start and end apart: 5, of which 2 were waited for; matrix products, arithmetic and copies ran while one was open for 4% of the time, Pallas kernels for 0%

profile of v1, /device:TPU:2, one launch (start us, length us, event | category | flops | bytes accessed | tf_op | source)
XLA Modules:
  0.0 206.5 jit_solution(9193807873951483971)
XLA Ops:
  6.5 0.0 all-gather.2.cloned.1.call-start
  6.5 0.0 copy-start.1
  6.5 0.9 copy-done.1
  7.5 0.0 copy-start.3
  7.5 0.7 copy-done.3
  8.1 0.6 ready.1
  8.8 1.6 collective-permute-start
  10.4 1.5 collective-permute-start.1
  11.9 2.2 %collective-permute-start.3 = (f32[48,8,128]{2,1,0:T(8,128)S(1)}, f32[48,8,128]{2,1,0:T(8,128)S(1)}, u32[]{:S(2)}, u32[]{:S(2)}) collective-permute-start(f32[48,8,128]{2,1,0:T(8,128)S(1)} %ready.1), channel_id=1, source_target_pairs={{0,24},{4,28},{8,0},{12,4},{16,8},{20,12},{24,16},{28,20},{1,25},{... | collective-permute-start | bytes 589832 | tf_op jit(solution)/shard_map/ppermute | solution.py:30
  14.2 8.0 %broadcast_in_dim.21.rest_refs_0_.rest_refs_1_.rest_refs_2_.rest_refs_3_.rest_refs_4_.rest_refs_5_.rest_refs_6_ = f32[48,7,128,128]{3,2,1,0:T(8,128)} broadcast(f32[48,7,128]{2,1,0:T(8,128)S(1)} %bitcast.16), dimensions={0,1,2} | broadcast | bytes 22192128 | tf_op jit(solution)/shard_map/broadcast_in_dim | solution.py:193
  22.2 0.5 collective-permute-start.2
  22.6 0.0 collective-permute-done
  22.7 0.0 collective-permute-done.1
  22.7 0.0 copy-start.6
  22.7 6.1 %collective-permute-done.2 = f32[48,8,128]{2,1,0:T(8,128)S(1)} collective-permute-done((f32[48,8,128]{2,1,0:T(8,128)S(1)}, f32[48,8,128]{2,1,0:T(8,128)S(1)}, u32[]{:S(2)}, u32[]{:S(2)}) %collective-permute-start.2) | collective-permute-done | bytes 196640 | tf_op jit(solution)/shard_map/ppermute | solution.py:30
  28.9 0.0 collective-permute-done.3
  28.9 0.0 copy-start.5
  28.9 0.9 copy-done.5
  29.9 0.0 all-gather.2.cloned.1.call-update
  29.9 0.0 copy-done.6
  29.9 0.0 copy-start.2
  29.9 0.0 copy-start.4
  29.9 0.1 copy.6
  30.0 0.6 convert_reduce_fusion
  30.6 0.2 select_reduce_fusion
  30.8 0.1 copy.8
  30.9 0.1 reshape.32.codes
  31.0 32.0 %all-gather.2.cloned.1.call-done = f32[5,192,8,128]{3,2,1,0:T(8,128)} async-done(((f32[5,48,8,128]{3,2,1,0:T(8,128)}), f32[5,192,8,128]{3,2,1,0:T(8,128)}) %all-gather.2.cloned.1.call-update) | async-done | bytes 3932176 | tf_op jit(solution)/shard_map/all_gather | solution.py:200
  63.0 2.9 %slice_compare_fusion = pred[960,1,128]{2,1,0:T(4,128)(4,1)S(1)} fusion(f32[960,8,128]{2,1,0:T(8,128)} %bitcast.14), kind=kLoop, calls=%fused_computation.3 | loop fusion | flops 122880 | bytes 614400 | tf_op jit(solution)/shard_map/gt | solution.py:205
  65.9 0.2 select_reduce_fusion.1.source_counts
  66.1 0.0 copy-done.2
  66.2 0.0 copy-done.4
  66.2 0.0 copy-start
  66.2 2.1 %copy-done = f32[5,192,8,128]{3,2,1,0:T(8,128)S(1)} copy-done((f32[5,192,8,128]{3,2,1,0:T(8,128)S(1)}, f32[5,192,8,128]{3,2,1,0:T(8,128)}, u32[]{:S(2)}) %copy-start) | copy-done | bytes 3932184
  68.3 131.3 %all_slabs.1 = f32[48,4,128]{2,1,0:T(4,128)} custom-call(s32[2160]{0:T(1024)S(1)} %reshape.32.codes, s32[48]{0:T(128)S(1)} %copy-done.4, s32[960]{0:T(1024)S(1)} %select_reduce_fusion.1.source_counts, f32[48,8,128]{2,1,0:T(8,128)S(1)} %ready.1, f32[960,8,128]{2,1,0:T(8,128)S(1)} %bitcast.15, ...), custom_call_target="tpu_custom_call" | custom-call | flops 2123366400 | bytes 3932160 | tf_op jit(solution)/shard_map/all_slabs/pallas_call | solution.py:207
  (7 shorter events, 0.1 us)
Async XLA Ops:
  6.5 56.5 %all-gather.2.cloned.1.call-start = ((), (), s32[]{:S(2)}) async-start(), calls=%async_computation | async-start | bytes 4915200 | tf_op jit(solution)/shard_map/all_gather | solution.py:200
  6.5 0.9 copy-start.1
  7.5 0.7 copy-start.3
  8.8 13.9 %collective-permute-start = (f32[48,8,128]{2,1,0:T(8,128)S(1)}, f32[48,8,128]{2,1,0:T(8,128)S(1)}, u32[]{:S(2)}, u32[]{:S(2)}) collective-permute-start(f32[48,8,128]{2,1,0:T(8,128)S(1)} %ready.1), channel_id=1, source_target_pairs={{0,8},{4,12},{8,16},{12,20},{16,24},{20,28},{24,0},{28,4},{1,9},{5... | collective-permute-start | bytes 589832 | tf_op jit(solution)/shard_map/ppermute | solution.py:30
  10.4 12.3 %collective-permute-start.1 = (f32[48,8,128]{2,1,0:T(8,128)S(1)}, f32[48,8,128]{2,1,0:T(8,128)S(1)}, u32[]{:S(2)}, u32[]{:S(2)}) collective-permute-start(f32[48,8,128]{2,1,0:T(8,128)S(1)} %ready.1), channel_id=1, source_target_pairs={{0,4},{4,8},{8,12},{12,16},{16,20},{20,24},{24,28},{28,0},{1,5},{5... | collective-permute-start | bytes 589832 | tf_op jit(solution)/shard_map/ppermute | solution.py:30
  11.9 16.9 %collective-permute-start.3 = (f32[48,8,128]{2,1,0:T(8,128)S(1)}, f32[48,8,128]{2,1,0:T(8,128)S(1)}, u32[]{:S(2)}, u32[]{:S(2)}) collective-permute-start(f32[48,8,128]{2,1,0:T(8,128)S(1)} %ready.1), channel_id=1, source_target_pairs={{0,24},{4,28},{8,0},{12,4},{16,8},{20,12},{24,16},{28,20},{1,25},{... | collective-permute-start | bytes 589832 | tf_op jit(solution)/shard_map/ppermute | solution.py:30
  22.2 6.7 %collective-permute-start.2 = (f32[48,8,128]{2,1,0:T(8,128)S(1)}, f32[48,8,128]{2,1,0:T(8,128)S(1)}, u32[]{:S(2)}, u32[]{:S(2)}) collective-permute-start(f32[48,8,128]{2,1,0:T(8,128)S(1)} %ready.1), channel_id=1, source_target_pairs={{0,28},{4,0},{8,4},{12,8},{16,12},{20,16},{24,20},{28,24},{1,29},{... | collective-permute-start | bytes 589832 | tf_op jit(solution)/shard_map/ppermute | solution.py:30
  22.7 7.2 %copy-start.6 = (s32[48,45]{1,0:T(8,128)S(1)}, s32[48,45]{1,0:T(8,128)}, u32[]{:S(2)}) copy-start(s32[48,45]{1,0:T(8,128)} %param.5) | copy-start | bytes 25924
  28.9 1.0 copy-start.5
  29.9 36.2 %copy-start.2 = (f32[48,8,128]{2,1,0:T(8,128)S(1)}, f32[48,8,128]{2,1,0:T(8,128)}, u32[]{:S(2)}) copy-start(f32[48,8,128]{2,1,0:T(8,128)} %rest_refs_7_.1) | copy-start | bytes 589828
  29.9 36.2 %copy-start.4 = (s32[48]{0:T(128)S(1)}, s32[48]{0:T(128)}, u32[]{:S(2)}) copy-start(s32[48]{0:T(128)} %live_counts.1) | copy-start | bytes 580
  66.2 2.1 %copy-start = (f32[5,192,8,128]{3,2,1,0:T(8,128)S(1)}, f32[5,192,8,128]{3,2,1,0:T(8,128)}, u32[]{:S(2)}) copy-start(f32[5,192,8,128]{3,2,1,0:T(8,128)} %all-gather.2.cloned.1.call-done) | copy-start | bytes 11796484
Sparse Core Ops, SparseCore 0:
  30.0 32.9 all-gather.1
